TPU v7x, 512 devices: a whole 4x4x16 slice. The times are simulated.
512 devices in a mesh: az: 64 (over x, z), rad: 4 (over y_lo, core), ax: 2 (over y_hi).
Axes of the slice: x: 4, y: 4 (y_hi: 2, y_lo: 2; y = y_hi * 2 + y_lo), z: 16, core: 2. Of those that a mesh axis runs over, the one named last changes fastest.
Arguments:
- state: bfloat16 [2, 6, 32, 1536, 512], P('ax', None, None, 'az', 'rad'), may hold values from -6 to 6
- diffusivity: bfloat16 [2, 32, 1536, 512], P('ax', None, 'az', 'rad'), may hold values from 0.019897461 to 0.15917969
- rotor_step: int32 [1], replicated, may hold values from 0 to 1535
Outputs:
- next_state: bfloat16 [2, 6, 32, 1536, 512], P('ax', None, None, 'az', 'rad')
All inputs are finite; a program needn't handle non-finite values.
Results may differ from a plain program's by a relative error of at most 0.006.
Values may be sent and summed in bfloat16 or wider, within the bound.
A program may use at most 64 MiB of HBM per device.

v0:
```python
import math

import jax
import jax.numpy as jnp
from jax import lax
from jax.sharding import PartitionSpec as P

CYCLE = 1536
MODES = 512


def from_partner(value, axis, apart):
    mask = 2**apart
    pairs = [(source, source ^ mask) for source in range(lax.axis_size(axis))]
    return lax.ppermute(value, axis, pairs)


def padded(x, sides, width, wrap):
    for axis, dim in sides:
        peers, length = (lax.axis_size(axis), x.shape[dim])
        up = [(i, (i + 1) % peers) for i in range(peers if wrap else peers - 1)]
        down = [(j, i) for i, j in up]
        last = lax.slice_in_dim(x, length - width, length, axis=dim)
        first = lax.slice_in_dim(x, 0, width, axis=dim)
        before = lax.ppermute(last, axis, up)
        after = lax.ppermute(first, axis, down)
        x = jnp.concatenate([before, x, after], axis=dim)
    return x


def angle_grid(first_count, second_count, cycle_cells):
    first_index = jnp.arange(first_count, dtype=jnp.int32)
    second_index = jnp.arange(second_count, dtype=jnp.int32)
    product_mod = jnp.mod(first_index[:, None] * second_index[None, :], cycle_cells)
    return product_mod.astype(jnp.float32) * (2.0 * math.pi / cycle_cells)


def forward_table(cycle_cells, mode_count):
    angles = angle_grid(cycle_cells, mode_count, cycle_cells)
    return jnp.concatenate([jnp.cos(angles), jnp.sin(angles)], axis=1).astype(jnp.bfloat16)


def inverse_table(cycle_cells, mode_count):
    angles = angle_grid(mode_count, cycle_cells, cycle_cells)
    mode_index = jnp.arange(mode_count, dtype=jnp.int32)
    weights = (jnp.where(mode_index == 0, 1.0, 2.0).astype(jnp.float32) / cycle_cells)[:, None]
    return jnp.concatenate([weights * jnp.cos(angles), weights * jnp.sin(angles)], axis=0).astype(
        jnp.bfloat16
    )


def rotate_modes(spectra, mode_count, cycle_cells, cell_shift):
    mode_index = jnp.arange(mode_count, dtype=jnp.int32)
    turned = jnp.mod(mode_index * cell_shift, cycle_cells).astype(jnp.float32) * (
        2.0 * math.pi / cycle_cells
    )
    cos_part = jnp.cos(turned)[None, :, None]
    sin_part = jnp.sin(turned)[None, :, None]
    cosine_part = spectra[:, :mode_count, :]
    sine_part = spectra[:, mode_count:, :]
    return jnp.concatenate(
        [
            cosine_part * cos_part - sine_part * sin_part,
            cosine_part * sin_part + sine_part * cos_part,
        ],
        axis=1,
    ).astype(jnp.bfloat16)


def body(state, diffusivity, rotor_step):
    side_index = lax.axis_index("ax")
    cell_shift = (1 - 2 * side_index) * rotor_step[0]
    own_block = state[0]
    fields, planes, sector, band_cells = own_block.shape
    cycle_rows = own_block.reshape(fields * planes, sector, band_cells)
    cycle_table = forward_table(CYCLE, MODES)
    back_table = inverse_table(CYCLE, MODES)
    spectra = jnp.einsum(
        "gar,ak->gkr",
        lax.all_to_all(cycle_rows, "az", split_axis=0, concat_axis=1, tiled=True),
        cycle_table,
        preferred_element_type=jnp.float32,
    )
    rebuilt = jnp.einsum(
        "gkr,ka->gar",
        rotate_modes(spectra, MODES, CYCLE, cell_shift),
        back_table,
        preferred_element_type=jnp.float32,
    )
    rebuilt_rows = rebuilt.astype(jnp.bfloat16)
    arrived = from_partner(rebuilt_rows, "ax", 0)
    carried = lax.all_to_all(arrived, "az", split_axis=1, concat_axis=0, tiled=True).reshape(
        fields, planes, sector, band_cells
    )
    own_coeff = diffusivity[0]
    stacked = jnp.concatenate([own_block, own_coeff[None]], axis=0)
    beside_all = padded(stacked, (("az", 2),), 1, True)
    beside = padded(stacked, (("rad", 3),), 1, False)
    values = own_block.astype(jnp.float32)
    coeffs = own_coeff.astype(jnp.float32)
    value_pad = jnp.pad(values, ((0, 0), (1, 1), (0, 0), (0, 0)))
    coeff_pad = jnp.pad(coeffs, ((1, 1), (0, 0), (0, 0)))
    neighbours = [
        (beside_all[:fields, :, 2:, :], beside_all[fields, :, 2:, :]),
        (beside_all[:fields, :, :-2, :], beside_all[fields, :, :-2, :]),
        (beside[:fields, :, :, 2:], beside[fields, :, :, 2:]),
        (beside[:fields, :, :, :-2], beside[fields, :, :, :-2]),
    ]
    flux_sum = jnp.zeros_like(values)
    for near_value, near_coeff in neighbours:
        flux_sum = flux_sum + 0.5 * (coeffs + near_coeff.astype(jnp.float32))[None] * (
            near_value.astype(jnp.float32) - values
        )
    flux_sum = flux_sum + 0.5 * (coeffs + coeff_pad[2:])[None] * (value_pad[:, 2:] - values)
    flux_sum = flux_sum + 0.5 * (coeffs + coeff_pad[:-2])[None] * (value_pad[:, :-2] - values)
    plane_mid = (jnp.arange(planes, dtype=jnp.float32) + 0.5) / planes
    weight = jnp.where(side_index == 0, plane_mid, 1.0 - plane_mid)
    blended = (
        values + flux_sum + weight[None, :, None, None] * (carried.astype(jnp.float32) - values)
    )
    return blended.astype(jnp.bfloat16)[None]


def solution(mesh):
    return jax.shard_map(
        body,
        mesh=mesh,
        in_specs=(P("ax", None, None, "az", "rad"), P("ax", None, "az", "rad"), P()),
        out_specs=P("ax", None, None, "az", "rad"),
        check_vma=False,
    )
```

profile of v0, /device:TPU:6, one launch (start us, length us, event | category | flops | bytes accessed | tf_op | source)
XLA Modules:
  0.0 216.6 jit_solution(15054795791723797130)
XLA Ops:
  0.0 18.8 %all-to-all-start = ((bf16[192,24,128]{2,1,0:T(8,128)(2,1)}), bf16[192,24,128]{2,1,0:T(8,128)(2,1)S(1)}, u32[]{:S(2)}, u32[]{:S(2)}) async-start(bf16[192,24,128]{2,1,0:T(8,128)(2,1)} %bitcast.43), calls=%async_computation | async-start | bytes 2359296 | tf_op jit(solution)/shard_map/all_to_all | solution.py:80
  19.5 13.8 %sine_convert_fusion = (bf16[1536,512]{0,1:T(8,128)(2,1)S(1)}, bf16[1536,512]{0,1:T(8,128)(2,1)}) fusion(), kind=kLoop, calls=%fused_computation.22 | loop fusion | flops 8650752 | bytes 3145728 | tf_op jit(solution)/shard_map/convert.7
  33.3 14.4 %multiply_convert_fusion.1 = (bf16[512,1536]{0,1:T(8,128)(2,1)}, bf16[512,1536]{0,1:T(8,128)(2,1)}) fusion(f32[512]{0:T(512)S(1)} %select_multiply_fusion), kind=kLoop, calls=%fused_computation.28 | loop fusion | flops 10223616 | bytes 3147776 | tf_op jit(solution)/shard_map/convert.8
  47.7 30.6 %all-to-all-done = bf16[192,24,128]{2,1,0:T(8,128)(2,1)S(1)} async-done(((bf16[192,24,128]{2,1,0:T(8,128)(2,1)}), bf16[192,24,128]{2,1,0:T(8,128)(2,1)S(1)}, u32[]{:S(2)}, u32[]{:S(2)}) %all-to-all-start) | async-done | bytes 1179680 | tf_op jit(solution)/shard_map/all_to_all | solution.py:80
  78.6 1.2 copy-done.8
  79.8 1.8 fusion.32
  83.0 1.8 fusion.17
  84.8 5.2 %collective-permute-start.4 = (bf16[3,1536,128]{2,1,0:T(8,128)(2,1)S(1)}, bf16[3,1536,128]{2,1,0:T(8,128)(2,1)S(1)}, u32[]{:S(2)}, u32[]{:S(2)}) collective-permute-start(bf16[3,1536,128]{2,1,0:T(8,128)(2,1)S(1)} %fusion.17), channel_id=1, source_target_pairs={{0,1},{1,0},{2,3},{3,2},{4,5},{5,4},{6,7},{7,6},{8,9},{9,8},{10,11... | collective-permute-start | bytes 3538952 | tf_op jit(solution)/shard_map/ppermute | solution.py:15
  90.1 21.5 %collective-permute-done.4 = bf16[3,1536,128]{2,1,0:T(8,128)(2,1)S(1)} collective-permute-done((bf16[3,1536,128]{2,1,0:T(8,128)(2,1)S(1)}, bf16[3,1536,128]{2,1,0:T(8,128)(2,1)S(1)}, u32[]{:S(2)}, u32[]{:S(2)}) %collective-permute-start.4) | collective-permute-done | bytes 1179680 | tf_op jit(solution)/shard_map/ppermute | solution.py:15
  111.6 8.2 %copy.24 = bf16[3,1536,128]{2,0,1:T(4,128)(2,1)} copy(bf16[3,1536,128]{2,1,0:T(8,128)(2,1)S(1)} %collective-permute-done.4) | data formatting | bytes 2359296 | tf_op jit(solution)/shard_map/ppermute | solution.py:15
  119.8 11.3 %all-to-all-start.1 = ((bf16[3,1536,128]{2,0,1:T(4,128)(2,1)}), bf16[3,1536,128]{2,0,1:T(4,128)(2,1)}, u32[]{:S(2)}, u32[]{:S(2)}) async-start(bf16[3,1536,128]{2,0,1:T(4,128)(2,1)} %copy.24), calls=%async_computation.1 | async-start | bytes 3145728 | tf_op jit(solution)/shard_map/all_to_all | solution.py:92
  131.1 1.7 slice_maximum_fusion
  132.8 2.4 %copy.19 = bf16[7,32,24,1]{1,2,3,0:T(8,128)(2,1)S(1)} copy(bf16[7,32,24,1]{3,2,1,0:T(8,128)(2,1)} %get-tuple-element.13) | data formatting | bytes 21504 | tf_op jit(solution)/shard_map/slice | solution.py:24
  135.2 1.3 collective-permute-start.2
  137.6 3.0 %collective-permute-start.3 = (bf16[7,32,24,1]{1,2,3,0:T(8,128)(2,1)S(1)}, bf16[7,32,24,1]{1,2,3,0:T(8,128)(2,1)S(1)}, u32[]{:S(2)}, u32[]{:S(2)}) collective-permute-start(bf16[7,32,24,1]{1,2,3,0:T(8,128)(2,1)S(1)} %copy.21), channel_id=1, source_target_pairs={{0,2},{2,4},{4,6},{1,3},{3,5},{5,7},{8,10},{10,12},{12,14},{9,11},... | collective-permute-start | bytes 32264 | tf_op jit(solution)/shard_map/ppermute | solution.py:25
  140.9 4.9 %collective-permute-start = (bf16[7,32,1,128]{3,2,1,0:T(2,128)(2,1)S(1)}, bf16[7,32,1,128]{3,2,1,0:T(2,128)(2,1)S(1)}, u32[]{:S(2)}, u32[]{:S(2)}) collective-permute-start(bf16[7,32,1,128]{3,2,1,0:T(2,128)(2,1)S(1)} %get-tuple-element.11), channel_id=1, source_target_pairs={{8,0},{16,8},{24,16},{32,24},{40,32},{48,40},{56,48},{64,56},{72,6... | collective-permute-start | bytes 172040 | tf_op jit(solution)/shard_map/ppermute | solution.py:26
  145.8 1.9 collective-permute-start.1
  148.7 1.6 bitcast_convert_fusion
  151.4 2.2 %copy.22 = bf16[7,32,24,1]{3,2,1,0:T(8,128)(2,1)} copy(bf16[7,32,24,1]{1,2,3,0:T(8,128)(2,1)S(1)} %collective-permute-done.3) | data formatting | bytes 21504 | tf_op jit(solution)/shard_map/ppermute | solution.py:25
  153.7 47.3 %collective-permute-done = bf16[7,32,1,128]{3,2,1,0:T(2,128)(2,1)S(1)} collective-permute-done((bf16[7,32,1,128]{3,2,1,0:T(2,128)(2,1)S(1)}, bf16[7,32,1,128]{3,2,1,0:T(2,128)(2,1)S(1)}, u32[]{:S(2)}, u32[]{:S(2)}) %collective-permute-start) | collective-permute-done | bytes 57376 | tf_op jit(solution)/shard_map/ppermute | solution.py:26
  201.9 2.3 %fusion.42 = (f32[32,24,128]{2,1,0:T(8,128)S(1)}, f32[32,24,128]{2,1,0:T(8,128)S(1)}, f32[32,24,128]{2,1,0:T(8,128)}, f32[32,24,128]{2,1,0:T(8,128)}) fusion(bf16[1,32,24,128]{3,2,1,0:T(8,128)(2,1)S(1)} %copy-done.3, bf16[7,32,1,128]{3,2,1,0:T(2,128)(2,1)} %copy-done.11, bf16[6,32,24,128]{3,2,1,0:T(8,128)(2,1)S(1)} %bitcast.46, ...), kind=kLoop, calls=%fused_computation.82 | loop fusion | flops 3244032 | bytes 3085312 | tf_op jit(solution)/shard_map/mul | solution.py:111
  204.1 1.9 all-to-all-done.1
  206.0 1.6 copy.25
  210.1 6.5 %fusion.33 = bf16[1,6,32,24,128]{4,3,2,1,0:T(8,128)(2,1)} fusion(f32[6,32,24,128]{3,2,1,0:T(8,128)S(1)} %bitcast.48, f32[32]{0:T(128)S(1)} %broadcast_select_fusion, f32[6,32,24,128]{3,2,1,0:T(8,128)S(1)} %copy-done.2, f32[32,24,128]{2,1,0:T(8,128)S(1)} %copy-done.7, f32[32,24,128]{2,1,0:T(8,128)S(1)} %copy-done.6, ...), kind=kLoop, calls=%fused_computation.64 | loop fusion | flops 27721728 | bytes 9770112 | tf_op jit(solution)/shard_map/broadcast_in_dim | solution.py:121
  (40 shorter events, 8.4 us)
Async XLA Ops:
  0.0 78.4 %all-to-all-start = ((bf16[192,24,128]{2,1,0:T(8,128)(2,1)}), bf16[192,24,128]{2,1,0:T(8,128)(2,1)S(1)}, u32[]{:S(2)}, u32[]{:S(2)}) async-start(bf16[192,24,128]{2,1,0:T(8,128)(2,1)} %bitcast.43), calls=%async_computation | async-start | bytes 2359296 | tf_op jit(solution)/shard_map/all_to_all | solution.py:80
  78.4 1.4 copy-start.8
  79.8 2.1 copy-start.10
  81.6 1.4 copy-start.9
  84.8 46.3 %copy-start = (bf16[1,6,32,24,128]{4,3,2,1,0:T(8,128)(2,1)S(1)}, bf16[1,6,32,24,128]{4,3,2,1,0:T(8,128)(2,1)}, u32[]{:S(2)}) copy-start(bf16[1,6,32,24,128]{4,3,2,1,0:T(8,128)(2,1)} %param.3) | copy-start | bytes 3538948
  84.8 46.3 %copy-start.3 = (bf16[1,32,24,128]{3,2,1,0:T(8,128)(2,1)S(1)}, bf16[1,32,24,128]{3,2,1,0:T(8,128)(2,1)}, u32[]{:S(2)}) copy-start(bf16[1,32,24,128]{3,2,1,0:T(8,128)(2,1)} %param.4) | copy-start | bytes 589828
  84.8 26.8 %collective-permute-start.4 = (bf16[3,1536,128]{2,1,0:T(8,128)(2,1)S(1)}, bf16[3,1536,128]{2,1,0:T(8,128)(2,1)S(1)}, u32[]{:S(2)}, u32[]{:S(2)}) collective-permute-start(bf16[3,1536,128]{2,1,0:T(8,128)(2,1)S(1)} %fusion.17), channel_id=1, source_target_pairs={{0,1},{1,0},{2,3},{3,2},{4,5},{5,4},{6,7},{7,6},{8,9},{9,8},{10,11... | collective-permute-start | bytes 3538952 | tf_op jit(solution)/shard_map/ppermute | solution.py:15
  119.8 86.2 %all-to-all-start.1 = ((bf16[3,1536,128]{2,0,1:T(4,128)(2,1)}), bf16[3,1536,128]{2,0,1:T(4,128)(2,1)}, u32[]{:S(2)}, u32[]{:S(2)}) async-start(bf16[3,1536,128]{2,0,1:T(4,128)(2,1)} %copy.24), calls=%async_computation.1 | async-start | bytes 3145728 | tf_op jit(solution)/shard_map/all_to_all | solution.py:92
  135.2 15.0 %collective-permute-start.2 = (bf16[7,32,24,1]{1,2,3,0:T(8,128)(2,1)S(1)}, bf16[7,32,24,1]{1,2,3,0:T(8,128)(2,1)S(1)}, u32[]{:S(2)}, u32[]{:S(2)}) collective-permute-start(bf16[7,32,24,1]{1,2,3,0:T(8,128)(2,1)S(1)} %copy.19), channel_id=1, source_target_pairs={{2,0},{4,2},{6,4},{3,1},{5,3},{7,5},{10,8},{12,10},{14,12},{11,9},... | collective-permute-start | bytes 32264 | tf_op jit(solution)/shard_map/ppermute | solution.py:26
  137.6 13.8 %collective-permute-start.3 = (bf16[7,32,24,1]{1,2,3,0:T(8,128)(2,1)S(1)}, bf16[7,32,24,1]{1,2,3,0:T(8,128)(2,1)S(1)}, u32[]{:S(2)}, u32[]{:S(2)}) collective-permute-start(bf16[7,32,24,1]{1,2,3,0:T(8,128)(2,1)S(1)} %copy.21), channel_id=1, source_target_pairs={{0,2},{2,4},{4,6},{1,3},{3,5},{5,7},{8,10},{10,12},{12,14},{9,11},... | collective-permute-start | bytes 32264 | tf_op jit(solution)/shard_map/ppermute | solution.py:25
  140.9 60.1 %collective-permute-start = (bf16[7,32,1,128]{3,2,1,0:T(2,128)(2,1)S(1)}, bf16[7,32,1,128]{3,2,1,0:T(2,128)(2,1)S(1)}, u32[]{:S(2)}, u32[]{:S(2)}) collective-permute-start(bf16[7,32,1,128]{3,2,1,0:T(2,128)(2,1)S(1)} %get-tuple-element.11), channel_id=1, source_target_pairs={{8,0},{16,8},{24,16},{32,24},{40,32},{48,40},{56,48},{64,56},{72,6... | collective-permute-start | bytes 172040 | tf_op jit(solution)/shard_map/ppermute | solution.py:26
  145.8 56.1 %collective-permute-start.1 = (bf16[7,32,1,128]{3,2,1,0:T(2,128)(2,1)S(1)}, bf16[7,32,1,128]{3,2,1,0:T(2,128)(2,1)}, u32[]{:S(2)}, u32[]{:S(2)}) collective-permute-start(bf16[7,32,1,128]{3,2,1,0:T(2,128)(2,1)S(1)} %get-tuple-element.12), channel_id=1, source_target_pairs={{0,8},{8,16},{16,24},{24,32},{32,40},{40,48},{48,56},{56,64},{64,7... | collective-permute-start | bytes 172040 | tf_op jit(solution)/shard_map/ppermute | solution.py:25
  201.0 0.6 copy-start.11
  207.6 1.0 copy-start.6
  207.6 1.1 copy-start.7
  207.8 1.4 copy-start.1
  207.8 2.2 %copy-start.2 = (f32[6,32,24,128]{3,2,1,0:T(8,128)S(1)}, f32[6,32,24,128]{3,2,1,0:T(8,128)}, u32[]{:S(2)}) copy-start(f32[6,32,24,128]{3,2,1,0:T(8,128)} %bitcast_convert_fusion) | copy-start | bytes 7077892
  207.8 2.2 %copy-start.4 = (f32[32,24,128]{2,1,0:T(8,128)S(1)}, f32[32,24,128]{2,1,0:T(8,128)}, u32[]{:S(2)}) copy-start(f32[32,24,128]{2,1,0:T(8,128)} %get-tuple-element.9) | copy-start | bytes 1179652
  207.8 2.3 %copy-start.5 = (f32[32,24,128]{2,1,0:T(8,128)S(1)}, f32[32,24,128]{2,1,0:T(8,128)}, u32[]{:S(2)}) copy-start(f32[32,24,128]{2,1,0:T(8,128)} %get-tuple-element.10) | copy-start | bytes 1179652
  207.8 2.3 %copy-start.12 = (bf16[7,32,1,128]{3,2,1,0:T(2,128)(2,1)S(1)}, bf16[7,32,1,128]{3,2,1,0:T(2,128)(2,1)}, u32[]{:S(2)}) copy-start(bf16[7,32,1,128]{3,2,1,0:T(2,128)(2,1)} %copy-done.11) | copy-start | bytes 172036
where the time goes:
time: 218 us; the launch traced here: 217 us
  waiting for transfers between devices  102 us (47%)
  starting transfers between devices  46.4 us (21%)
  other arithmetic  42 us (19%)
  local copies, waits for them, and re-layouts  22.1 us (10%)
  matrix products  3.61 us (2%)
    ppermute x2, waiting for transfers between devices, padded(): after = lax.ppermute(first, axis, down)  47.3 us
    all_to_all x1, waiting for transfers between devices, body(): lax.all_to_all(cycle_rows, 'az', split_axis=0, concat_axis=1, tiled=True)  30.6 us
    another operation x3, other arithmetic  28.5 us
    ppermute x1, waiting for transfers between devices, from_partner(): return lax.ppermute(value, axis, pairs)  21.5 us
    all_to_all x1, starting transfers between devices, body(): lax.all_to_all(cycle_rows, 'az', split_axis=0, concat_axis=1, tiled=True)  18.8 us
    all_to_all x1, starting transfers between devices, body(): lax.all_to_all(arrived, 'az', split_axis=1, concat_axis=0, tiled=True)  11.3 us
    ppermute x1, local copies, waits for them, and re-layouts, from_partner(): return lax.ppermute(value, axis, pairs)  8.21 us
    broadcast_in_dim x1, other arithmetic, body(): return blended.astype(jnp.bfloat16)[None]  6.46 us
  transfers between devices with their start and end apart: 7, of which 5 were waited for; matrix products, arithmetic and copies ran while one was open for 19% of the time, Pallas kernels for 0%

commit v1 on v0

v1 whole, which is shorter than its diff:
```python
import math

import jax
import jax.numpy as jnp
from jax import lax
from jax.experimental import pallas as pl
from jax.experimental.pallas import tpu as pltpu
from jax.sharding import PartitionSpec as P

CYCLE = 1536
MODES = 512
FIELDS = 6
PLANES = 32
ROWS = FIELDS * PLANES
CELLS = 24
LANES = 128
RING = 64
COLS = 16
PARTS = 3
GROUP = 8
MESH = pl.DeviceIdType.MESH
F32 = jnp.float32
BF16 = jnp.bfloat16


def iota(shape, dim):
    return lax.broadcasted_iota(jnp.int32, shape, dim)


def wrapped(product):
    left = product - jnp.floor(product * (1.0 / CYCLE)) * float(CYCLE)
    left = jnp.where(left < 0.0, left + float(CYCLE), left)
    return jnp.where(left >= float(CYCLE), left - float(CYCLE), left)


def cos_sin(cells):
    quarter = jnp.floor(cells * (4.0 / CYCLE) + 0.5)
    t = (cells - quarter * (CYCLE / 4.0)) * (2.0 * math.pi / CYCLE)
    u = t * t
    sine = t * (1.0 + u * (-1.0 / 6 + u * (1.0 / 120 + u * (-1.0 / 5040 + u * (1.0 / 362880)))))
    cosine = 1.0 + u * (-0.5 + u * (1.0 / 24 + u * (-1.0 / 720 + u * (1.0 / 40320 - u * (1.0 / 3628800)))))
    odd = (quarter == 1.0) | (quarter == 3.0)
    c = jnp.where(odd, sine, cosine)
    s = jnp.where(odd, cosine, sine)
    c = jnp.where((quarter == 1.0) | (quarter == 2.0), -c, c)
    s = jnp.where((quarter == 2.0) | (quarter == 3.0), -s, s)
    return c, s


def kernel(
    state,
    diffusivity,
    rotor_step,
    out,
    cycles,
    rebuilt,
    carried,
    base,
    forward,
    back,
    spun,
    phase,
    fine,
    coarse,
    edge_rows,
    near_rows,
    near_rows32,
    edge_cols,
    near_cols,
    near_cols_t,
    face_x,
    face,
    send1,
    recv1,
    send2,
    recv2,
    send_h,
    recv_h,
):
    az, rad, ax = lax.axis_index("az"), lax.axis_index("rad"), lax.axis_index("ax")
    x, z = az // COLS, lax.rem(az, COLS)
    az_up, az_down = lax.rem(az + 1, RING), lax.rem(az + RING - 1, RING)
    rad_up, rad_down = lax.rem(rad + 1, 4), lax.rem(rad + 3, 4)

    def partner(k):
        m = k // 4
        far = (m + 1) // 2
        dz = jnp.where(lax.rem(m, 2) == 1, far, COLS - far)
        return lax.rem(x + lax.rem(k, 4), 4) * COLS + lax.rem(z + dz, COLS)

    barrier = pltpu.get_barrier_semaphore()

    def greet(k, carry):
        pl.semaphore_signal(barrier, inc=1, device_id=(partner(k), rad, 1 - ax), device_id_type=MESH)

        @pl.when(k > 0)
        def _():
            pl.semaphore_signal(barrier, inc=1, device_id=(partner(k), rad, ax), device_id_type=MESH)

        return carry

    lax.fori_loop(0, RING, greet, 0)
    pl.semaphore_signal(barrier, inc=1, device_id=(az, rad_up, ax), device_id_type=MESH)
    pl.semaphore_signal(barrier, inc=1, device_id=(az, rad_down, ax), device_id_type=MESH)
    pl.semaphore_wait(barrier, 2 * RING + 1)

    for part in range(PARTS):

        def send(k, carry, part=part):
            j = partner(k)
            pltpu.make_async_remote_copy(
                src_ref=state.at[part * RING + j],
                dst_ref=cycles.at[part, az],
                send_sem=send1.at[part],
                recv_sem=recv1.at[part],
                device_id=(j, rad, 1 - ax),
                device_id_type=MESH,
            ).start()
            return carry

        lax.fori_loop(0, RING, send, 0)

    def edges(ref, i, slot, acc):
        block = ref[pl.ds(pl.multiple_of(i * 16, 16), 16)]
        wide = block.astype(F32)
        rows = pl.ds(pl.multiple_of(slot * 16, 16), 16)
        edge_rows[0, rows, :] = wide[:, 0, :].astype(BF16)
        edge_rows[1, rows, :] = wide[:, CELLS - 1, :].astype(BF16)
        row, lane = iota((32, LANES), 0), iota((32, LANES), 1)
        pick = ((row == slot) & (lane == 0)) | ((row == slot + 16) & (lane == LANES - 1))
        return acc + lax.dot_general(
            jnp.where(pick, 1.0, 0.0).astype(BF16),
            block.reshape(16 * CELLS, LANES),
            (((1,), (1,)), ((), ())),
            preferred_element_type=F32,
        )

    acc = jnp.zeros((32, 16 * CELLS), F32)
    acc = lax.fori_loop(0, ROWS // 16, lambda i, a: edges(state, i, i, a), acc)
    acc = lax.fori_loop(0, PLANES // 16, lambda i, a: edges(diffusivity, i, i + ROWS // 16, a), acc)
    edge_cols[0] = acc[:16].astype(BF16)
    edge_cols[1] = acc[16:].astype(BF16)

    def halo(n, src, dst, target):
        return pltpu.make_async_remote_copy(
            src_ref=src, dst_ref=dst, send_sem=send_h.at[n], recv_sem=recv_h.at[n],
            device_id=target, device_id_type=MESH,
        )

    halos = [
        halo(0, edge_rows.at[1], near_rows.at[0], (az_up, rad, ax)),
        halo(1, edge_rows.at[0], near_rows.at[1], (az_down, rad, ax)),
        halo(2, edge_cols.at[1], near_cols.at[0], (az, rad_up, ax)),
        halo(3, edge_cols.at[0], near_cols.at[1], (az, rad_down, ax)),
    ]
    for copy in halos:
        copy.start()

    def grid(first, rows, columns):
        a = iota((rows, columns), 0).astype(F32)
        b = iota((rows, columns), 1).astype(F32)
        return cos_sin(wrapped(first * a * b))

    fine[0], fine[1] = grid(1.0, 16, CYCLE)
    coarse[0], coarse[1] = grid(16.0, MODES // 16, CYCLE)

    def forward_rows(i, carry):
        c0, s0 = fine[0], fine[1]
        c1, s1 = coarse[0, pl.ds(i, 1), :], coarse[1, pl.ds(i, 1), :]
        forward[pl.ds(pl.multiple_of(i * 16, 16), 16), :] = (c1 * c0 - s1 * s0).astype(BF16)
        forward[pl.ds(pl.multiple_of(MODES + i * 16, 16), 16), :] = (s1 * c0 + c1 * s0).astype(BF16)
        return carry

    lax.fori_loop(0, MODES // 16, forward_rows, 0)

    weight_k = jnp.where(iota((16, MODES), 1) == 0, 1.0, 2.0).astype(F32) / CYCLE
    fine[0, :, :MODES] = fine[0, :, :MODES] * weight_k
    fine[1, :, :MODES] = fine[1, :, :MODES] * weight_k
    c, s = grid(16.0, CYCLE // 16, MODES)
    for n in range(3):
        coarse[0, :, n * MODES : (n + 1) * MODES] = c[n * 32 : (n + 1) * 32]
        coarse[1, :, n * MODES : (n + 1) * MODES] = s[n * 32 : (n + 1) * 32]
    for n in range(3):

        def back_rows(i, carry, n=n):
            c0, s0 = fine[0, :, :MODES], fine[1, :, :MODES]
            c1 = coarse[0, pl.ds(i, 1), n * MODES : (n + 1) * MODES]
            s1 = coarse[1, pl.ds(i, 1), n * MODES : (n + 1) * MODES]
            rows = pl.ds(pl.multiple_of((n * 32 + i) * 16, 16), 16)
            back[rows, :MODES] = (c1 * c0 - s1 * s0).astype(BF16)
            back[rows, MODES:] = (s1 * c0 + c1 * s0).astype(BF16)
            return carry

        lax.fori_loop(0, 32, back_rows, 0)

    shift = ((2 * ax - 1) * rotor_step[0]).astype(F32)
    phase[0], phase[1] = cos_sin(wrapped(iota((MODES, LANES), 0).astype(F32) * shift))

    def transform(part):
        pltpu.make_async_copy(cycles.at[part], cycles.at[part], recv1.at[part]).wait()
        step = MODES // 2

        def ahead(i, carry):
            rows = pl.ds(pl.multiple_of(i * step, step), step)
            sine_rows = pl.ds(pl.multiple_of(MODES + i * step, step), step)
            cells = cycles[part].reshape(CYCLE, LANES)
            c = jnp.dot(forward[rows, :], cells, preferred_element_type=F32)
            d = jnp.dot(forward[sine_rows, :], cells, preferred_element_type=F32)
            cos_p, sin_p = phase[0, rows, :], phase[1, rows, :]
            spun[rows, :] = (c * cos_p - d * sin_p).astype(BF16)
            spun[sine_rows, :] = (c * sin_p + d * cos_p).astype(BF16)
            return carry

        lax.fori_loop(0, 2, ahead, 0)

        def astern(i, carry):
            rows = pl.ds(pl.multiple_of(i * (CYCLE // 4), CYCLE // 4), CYCLE // 4)
            cells = jnp.dot(back[rows, :], spun[...], preferred_element_type=F32).astype(BF16)
            rebuilt[part, pl.ds(i * COLS, COLS)] = cells.reshape(COLS, CELLS, LANES)
            return carry

        lax.fori_loop(0, 4, astern, 0)
        pltpu.make_async_copy(rebuilt.at[part, az], carried.at[part, az], recv2.at[part]).start()

        def send(k, carry):
            j = partner(k)
            pltpu.make_async_remote_copy(
                src_ref=rebuilt.at[part, j],
                dst_ref=carried.at[part, az],
                send_sem=send2.at[part],
                recv_sem=recv2.at[part],
                device_id=(j, rad, ax),
                device_id_type=MESH,
            ).start()
            return carry

        lax.fori_loop(1, RING, send, 0)

    lane = iota((GROUP, CELLS, LANES), 2)
    cell = iota((GROUP, CELLS, LANES), 1)

    def around(ref, i, slot, last):
        here = ref[pl.ds(i * GROUP, GROUP)].astype(F32)
        below = ref[pl.ds(jnp.maximum(i * GROUP - 1, 0), 1)].astype(F32)
        above = ref[pl.ds(jnp.minimum(i * GROUP + GROUP, last), 1)].astype(F32)
        plane_down = jnp.concatenate([below, here[:-1]], axis=0)
        plane_up = jnp.concatenate([here[1:], above], axis=0)
        rows = pl.ds(pl.multiple_of(slot * GROUP, GROUP), GROUP)
        cell_down = jnp.where(cell == 0, near_rows32[0, rows, :][:, None, :], pltpu.roll(here, 1, 1))
        cell_up = jnp.where(cell == CELLS - 1, near_rows32[1, rows, :][:, None, :], pltpu.roll(here, CELLS - 1, 1))
        half = lax.rem(slot, 2) * (GROUP * CELLS)
        columns = near_cols_t[pl.ds(pl.multiple_of(half, GROUP * CELLS), GROUP * CELLS), :].astype(BF16)
        pair = slot // 2
        r, l = iota((32, LANES), 0), iota((32, LANES), 1)
        place = ((r == pair) & (l == 0)) | ((r == pair + 16) & (l == LANES - 1))
        beyond = jnp.dot(columns, jnp.where(place, 1.0, 0.0).astype(BF16), preferred_element_type=F32)
        beyond = beyond.reshape(GROUP, CELLS, LANES)
        radius_down = jnp.where(lane == 0, beyond, pltpu.roll(here, 1, 2))
        radius_up = jnp.where(lane == LANES - 1, beyond, pltpu.roll(here, LANES - 1, 2))
        return here, plane_down, plane_up, cell_down, cell_up, radius_down, radius_up

    def side_weight(plane):
        middle = (plane.astype(F32) + 0.5) / PLANES
        return jnp.where(ax == 0, middle, 1.0 - middle)

    def faces(i, carry):
        here, plane_down, plane_up, *others = around(diffusivity, i, ROWS // GROUP + i, PLANES - 1)
        plane = iota((GROUP, CELLS, LANES), 0) + i * GROUP
        planes = pl.ds(i * GROUP, GROUP)
        first, final = plane == 0, plane == PLANES - 1
        down = 0.5 * (here + jnp.where(first, 0.0, plane_down))
        up = 0.5 * (here + jnp.where(final, 0.0, plane_up))
        total = down + up
        face_x[0, planes] = jnp.where(first, 0.0, down)
        face_x[1, planes] = jnp.where(final, 0.0, up)
        for n, other in enumerate(others):
            between = 0.5 * (here + other)
            face[n, planes] = between
            total = total + between
        face[4, planes] = 1.0 - total - side_weight(plane)
        return carry

    def flux(i, carry):
        here, plane_down, plane_up, *others = around(state, i, i, ROWS - 1)
        planes = pl.ds(lax.rem(i, PLANES // GROUP) * GROUP, GROUP)
        total = face[4, planes] * here
        total = total + face_x[0, planes] * plane_down
        total = total + face_x[1, planes] * plane_up
        for n, other in enumerate(others):
            total = total + face[n, planes] * other
        base[pl.ds(i * GROUP, GROUP)] = total
        return carry

    def blend(part):
        pltpu.make_async_copy(carried.at[part], carried.at[part], recv2.at[part]).wait()

        def some(i, carry):
            weight = side_weight(lax.rem(i, PLANES // GROUP) * GROUP + iota((GROUP, CELLS, LANES), 0))
            rows = pl.ds(part * RING + i * GROUP, GROUP)
            out[rows] = (base[rows] + weight * carried[part, pl.ds(i * GROUP, GROUP)].astype(F32)).astype(BF16)
            return carry

        lax.fori_loop(0, RING // GROUP, some, 0)

    transform(0)

    for copy in halos:
        copy.wait()

    def widen(i, carry):
        rows = pl.ds(pl.multiple_of(i * 16, 16), 16)
        near_rows32[0, rows, :] = near_rows[0, rows, :].astype(F32)
        near_rows32[1, rows, :] = near_rows[1, rows, :].astype(F32)
        return carry

    lax.fori_loop(0, (ROWS + PLANES) // 16, widen, 0)
    low = jnp.where(rad == 0, 0.0, near_cols[0].astype(F32))
    high = jnp.where(rad == 3, 0.0, near_cols[1].astype(F32))
    near_cols_t[...] = jnp.concatenate([low, high], axis=0).T
    lax.fori_loop(0, PLANES // GROUP, faces, 0)
    lax.fori_loop(0, ROWS // GROUP, flux, 0)

    for part in range(1, PARTS):
        transform(part)
    for part in range(PARTS):
        blend(part)
    for part in range(PARTS):
        pltpu.make_async_copy(cycles.at[part], cycles.at[part], send1.at[part]).wait()
        sent = rebuilt.at[part, pl.ds(0, RING - 1)]
        pltpu.make_async_copy(sent, sent, send2.at[part]).wait()


def body(state, diffusivity, rotor_step):
    vmem = pl.BlockSpec(memory_space=pltpu.VMEM)
    block = (PARTS, RING, CELLS, LANES)
    result = pl.pallas_call(
        kernel,
        out_shape=jax.ShapeDtypeStruct((ROWS, CELLS, LANES), BF16),
        in_specs=[vmem, vmem, pl.BlockSpec(memory_space=pltpu.SMEM)],
        out_specs=vmem,
        scratch_shapes=[
            pltpu.VMEM(block, BF16),
            pltpu.VMEM(block, BF16),
            pltpu.VMEM(block, BF16),
            pltpu.VMEM((ROWS, CELLS, LANES), F32),
            pltpu.VMEM((2 * MODES, CYCLE), BF16),
            pltpu.VMEM((CYCLE, 2 * MODES), BF16),
            pltpu.VMEM((2 * MODES, LANES), BF16),
            pltpu.VMEM((2, MODES, LANES), F32),
            pltpu.VMEM((2, 16, CYCLE), F32),
            pltpu.VMEM((2, MODES // 16, CYCLE), F32),
            pltpu.VMEM((2, ROWS + PLANES, LANES), BF16),
            pltpu.VMEM((2, ROWS + PLANES, LANES), BF16),
            pltpu.VMEM((2, ROWS + PLANES, LANES), F32),
            pltpu.VMEM((2, 16, 16 * CELLS), BF16),
            pltpu.VMEM((2, 16, 16 * CELLS), BF16),
            pltpu.VMEM((16 * CELLS, 32), F32),
            pltpu.VMEM((2, PLANES, CELLS, LANES), F32),
            pltpu.VMEM((5, PLANES, CELLS, LANES), F32),
            pltpu.SemaphoreType.DMA((PARTS,)),
            pltpu.SemaphoreType.DMA((PARTS,)),
            pltpu.SemaphoreType.DMA((PARTS,)),
            pltpu.SemaphoreType.DMA((PARTS,)),
            pltpu.SemaphoreType.DMA((4,)),
            pltpu.SemaphoreType.DMA((4,)),
        ],
        compiler_params=pltpu.CompilerParams(
            collective_id=0, has_side_effects=True, vmem_limit_bytes=48 * 1024 * 1024
        ),
    )(state.reshape(ROWS, CELLS, LANES), diffusivity.reshape(PLANES, CELLS, LANES), rotor_step)
    return result.reshape(1, FIELDS, PLANES, CELLS, LANES)


def solution(mesh):
    return jax.shard_map(
        body,
        mesh=mesh,
        in_specs=(P("ax", None, None, "az", "rad"), P("ax", None, "az", "rad"), P()),
        out_specs=P("ax", None, None, "az", "rad"),
        check_vma=False,
    )
```

time: 218 us -> 133 us (0.61)
  Pallas kernels: 0 us -> 129 us
  waiting for transfers between devices: 102 us -> 0 us
  starting transfers between devices: 46.4 us -> 0 us
  other arithmetic: 42 us -> 0 us
  local copies, waits for them, and re-layouts: 22.1 us -> 3.21 us
  matrix products: 3.61 us -> 0 us
    pallas_call x0 -> x1, Pallas kernels: none -> 129 us  [body(): pl.pallas_call(kernel, out_shape=jax.ShapeDtypeStruct((ROWS, CELLS, LANES...]
    ppermute x5 -> x0, waiting for transfers between devices: 69.1 us -> none  [the longest x2 47.3 us: padded(): after = lax.ppermute(first, axis, down)]
    all_to_all x2 -> x0, waiting for transfers between devices: 32.5 us -> none  [the longest x1 30.6 us: body(): lax.all_to_all(cycle_rows, 'az', split_axis=0, concat_axis=1, tiled=True)]
    all_to_all x2 -> x0, starting transfers between devices: 30.1 us -> none  [the longest x1 18.8 us: body(): lax.all_to_all(cycle_rows, 'az', split_axis=0, concat_axis=1, tiled=True)]
    another operation x3 -> x0, other arithmetic: 28.5 us -> none
    ppermute x5 -> x0, starting transfers between devices: 16.3 us -> none  [the longest x2 6.15 us: padded(): after = lax.ppermute(first, axis, down)]
    ppermute x3 -> x0, local copies, waits for them, and re-layouts: 11.6 us -> none  [the longest x1 8.21 us: from_partner(): return lax.ppermute(value, axis, pairs)]
    broadcast_in_dim x1 -> x0, other arithmetic: 6.46 us -> none  [body(): return blended.astype(jnp.bfloat16)[None]]
  transfers between devices with their start and end apart: 7 -> 0, of which waited for: 5 -> 0; matrix products, arithmetic and copies ran while one was open for 19% -> 0% of each run, Pallas kernels for 0% -> 0%
where the time goes in v1:
time: 133 us
  Pallas kernels  129 us (97%)
  local copies, waits for them, and re-layouts  3.21 us (2%)
    pallas_call x1, Pallas kernels, body(): pl.pallas_call(kernel, out_shape=jax.ShapeDtypeStruct((ROWS, CELLS, LANES...  129 us
    unnamed x5, local copies, waits for them, and re-layouts  3.21 us

profile of v1, /device:TPU:6, one launch (start us, length us, event | category | flops | bytes accessed | tf_op | source)
XLA Modules:
  0.0 132.5 jit_solution(653201601743305498)
XLA Ops:
  0.7 0.0 copy-start
  0.7 1.3 copy-done
  1.9 0.0 copy-start.1
  1.9 0.9 copy-done.1
  2.9 128.6 %shard_map.37 = bf16[192,24,128]{2,1,0:T(8,128)(2,1)S(1)} custom-call(bf16[192,24,128]{2,1,0:T(8,128)(2,1)S(1)} %bitcast.4, bf16[32,24,128]{2,1,0:T(8,128)(2,1)S(1)} %bitcast.5, s32[1]{0:T(128)S(6)} %copy.5.rotor_step), custom_call_target="tpu_custom_call" | custom-call | tf_op jit(solution)/shard_map/pallas_call | solution.py:336
  131.5 1.0 copy.6
Async XLA Ops:
  0.7 1.3 copy-start
  1.9 0.9 copy-start.1

commit v2 on v1

--- a/solution.py
+++ b/solution.py
@@ -1,3 +1,4 @@
+import functools
 import math
 
 import jax
@@ -16,6 +17,8 @@
 LANES = 128
 RING = 64
 COLS = 16
+FAR = COLS // 2
+NEAR = 5
 PARTS = 3
 GROUP = 8
 MESH = pl.DeviceIdType.MESH
@@ -48,8 +51,8 @@
 
 
 def kernel(
-    state,
-    diffusivity,
+    state_hbm,
+    diffusivity_hbm,
     rotor_step,
     out,
     cycles,
@@ -76,38 +79,51 @@
     recv2,
     send_h,
     recv_h,
+    state,
+    diffusivity,
+    load,
+    known_below,
+    known_above,
 ):
     az, rad, ax = lax.axis_index("az"), lax.axis_index("rad"), lax.axis_index("ax")
     x, z = az // COLS, lax.rem(az, COLS)
     az_up, az_down = lax.rem(az + 1, RING), lax.rem(az + RING - 1, RING)
     rad_up, rad_down = lax.rem(rad + 1, 4), lax.rem(rad + 3, 4)
 
-    def partner(k):
-        m = k // 4
-        far = (m + 1) // 2
-        dz = jnp.where(lax.rem(m, 2) == 1, far, COLS - far)
-        return lax.rem(x + lax.rem(k, 4), 4) * COLS + lax.rem(z + dz, COLS)
+    z_up, z_down = lax.rem(z + 1, COLS), lax.rem(z + COLS - 1, COLS)
+    loads = [
+        pltpu.make_async_copy(state_hbm, state, load.at[0]),
+        pltpu.make_async_copy(diffusivity_hbm, diffusivity, load.at[1]),
+    ]
+    for copy in loads:
+        copy.start()
+
+    def signal(semaphore, *device):
+        pl.semaphore_signal(semaphore, inc=1, device_id=device, device_id_type=MESH)
 
     barrier = pltpu.get_barrier_semaphore()
-
-    def greet(k, carry):
-        pl.semaphore_signal(barrier, inc=1, device_id=(partner(k), rad, 1 - ax), device_id_type=MESH)
-
-        @pl.when(k > 0)
-        def _():
-            pl.semaphore_signal(barrier, inc=1, device_id=(partner(k), rad, ax), device_id_type=MESH)
-
-        return carry
-
-    lax.fori_loop(0, RING, greet, 0)
-    pl.semaphore_signal(barrier, inc=1, device_id=(az, rad_up, ax), device_id_type=MESH)
-    pl.semaphore_signal(barrier, inc=1, device_id=(az, rad_down, ax), device_id_type=MESH)
-    pl.semaphore_wait(barrier, 2 * RING + 1)
-
-    for part in range(PARTS):
-
-        def send(k, carry, part=part):
-            j = partner(k)
+    for turn in range(4):
+        run = lax.rem(x + turn, 4) * COLS
+        for side in (ax, 1 - ax):
+            signal(barrier, run + z_up, rad, side)
+            signal(barrier, run + z_down, rad, side)
+        signal(barrier, run + z, rad, 1 - ax)
+        if turn:
+            signal(barrier, run + z, rad, ax)
+    signal(barrier, az, rad_up, ax)
+    signal(barrier, az, rad_down, ax)
+    pl.semaphore_wait(barrier, 25)
+    signal(known_below.at[2], x * COLS + z_up, rad, ax)
+    signal(known_above.at[2], x * COLS + z_down, rad, ax)
+    for copy in loads:
+        copy.wait()
+
+    def place(turn, dz):
+        return lax.rem(x + turn, 4) * COLS + lax.rem(z + dz, COLS)
+
+    def send_plane(first, count, dz):
+        def send(k, carry):
+            part, j = first + k // 4, place(lax.rem(k, 4), dz)
             pltpu.make_async_remote_copy(
                 src_ref=state.at[part * RING + j],
                 dst_ref=cycles.at[part, az],
@@ -118,7 +134,37 @@
             ).start()
             return carry
 
-        lax.fori_loop(0, RING, send, 0)
+        lax.fori_loop(0, 4 * count, send, 0)
+
+    def send_both(first, count, far):
+        send_plane(first, count, far)
+        send_plane(first, count, COLS - far)
+
+    send_plane(0, PARTS, 0)
+    send_both(0, PARTS, 1)
+
+    def reach(far, carry, count):
+        pl.semaphore_wait(known_below.at[far], 1)
+        signal(known_below.at[far + 1], x * COLS + z_up, rad, ax)
+        pl.semaphore_wait(known_above.at[far], 1)
+
+        @pl.when(far < FAR - 1)
+        def _():
+            signal(known_above.at[far + 1], x * COLS + z_down, rad, ax)
+
+        send_both(0, count, far)
+        return carry
+
+    lax.fori_loop(2, NEAR + 1, functools.partial(reach, count=PARTS), 0)
+    lax.fori_loop(NEAR + 1, FAR, functools.partial(reach, count=1), 0)
+    pl.semaphore_wait(known_below.at[FAR], 1)
+    send_plane(0, PARTS, FAR)
+
+    def send_rest(i, carry):
+        send_both(1 + i // (FAR - 1 - NEAR), 1, FAR - 1 - lax.rem(i, FAR - 1 - NEAR))
+        return carry
+
+    lax.fori_loop(0, (PARTS - 1) * (FAR - 1 - NEAR), send_rest, 0)
 
     def edges(ref, i, slot, acc):
         block = ref[pl.ds(pl.multiple_of(i * 16, 16), 16)]
@@ -223,7 +269,9 @@
         pltpu.make_async_copy(rebuilt.at[part, az], carried.at[part, az], recv2.at[part]).start()
 
         def send(k, carry):
-            j = partner(k)
+            m = COLS - 1 - k // 4
+            far = (m + 1) // 2
+            j = place(lax.rem(k, 4), jnp.where(lax.rem(m, 2) == 1, far, COLS - far))
             pltpu.make_async_remote_copy(
                 src_ref=rebuilt.at[part, j],
                 dst_ref=carried.at[part, az],
@@ -234,7 +282,8 @@
             ).start()
             return carry
 
-        lax.fori_loop(1, RING, send, 0)
+        lax.fori_loop(0, RING - 4, send, 0)
+        lax.fori_loop(RING - 3, RING, send, 0)
 
     lane = iota((GROUP, CELLS, LANES), 2)
     cell = iota((GROUP, CELLS, LANES), 1)
@@ -332,11 +381,12 @@
 
 def body(state, diffusivity, rotor_step):
     vmem = pl.BlockSpec(memory_space=pltpu.VMEM)
+    hbm = pl.BlockSpec(memory_space=pltpu.HBM)
     block = (PARTS, RING, CELLS, LANES)
     result = pl.pallas_call(
         kernel,
         out_shape=jax.ShapeDtypeStruct((ROWS, CELLS, LANES), BF16),
-        in_specs=[vmem, vmem, pl.BlockSpec(memory_space=pltpu.SMEM)],
+        in_specs=[hbm, hbm, pl.BlockSpec(memory_space=pltpu.SMEM)],
         out_specs=vmem,
         scratch_shapes=[
             pltpu.VMEM(block, BF16),
@@ -363,9 +413,14 @@
             pltpu.SemaphoreType.DMA((PARTS,)),
             pltpu.SemaphoreType.DMA((4,)),
             pltpu.SemaphoreType.DMA((4,)),
+            pltpu.VMEM((ROWS, CELLS, LANES), BF16),
+            pltpu.VMEM((PLANES, CELLS, LANES), BF16),
+            pltpu.SemaphoreType.DMA((2,)),
+            pltpu.SemaphoreType.REGULAR((FAR + 1,)),
+            pltpu.SemaphoreType.REGULAR((FAR + 1,)),
         ],
         compiler_params=pltpu.CompilerParams(
-            collective_id=0, has_side_effects=True, vmem_limit_bytes=48 * 1024 * 1024
+            collective_id=0, has_side_effects=True, vmem_limit_bytes=52 * 1024 * 1024
         ),
     )(state.reshape(ROWS, CELLS, LANES), diffusivity.reshape(PLANES, CELLS, LANES), rotor_step)
     return result.reshape(1, FIELDS, PLANES, CELLS, LANES)

time: 133 us -> 124 us (0.932)
  Pallas kernels: 129 us -> 120 us
    pallas_call x1, Pallas kernels: 129 us -> 120 us  [body(): pl.pallas_call(kernel, out_shape=jax.ShapeDtypeStruct((ROWS, CELLS, LANES...]
    unnamed x5 -> x3, local copies, waits for them, and re-layouts: 3.21 us -> 1.94 us
where the time goes in v2:
time: 124 us; the launch traced here: 123 us
  Pallas kernels  120 us (97%)
  local copies, waits for them, and re-layouts  1.94 us (2%)
    pallas_call x1, Pallas kernels, body(): pl.pallas_call(kernel, out_shape=jax.ShapeDtypeStruct((ROWS, CELLS, LANES...  120 us

profile of v2, /device:TPU:6, one launch (start us, length us, event | category | flops | bytes accessed | tf_op | source)
XLA Modules:
  0.0 122.9 jit_solution(12691373359225434947)
XLA Ops:
  0.7 0.0 copy-start
  0.7 0.9 copy-done
  1.6 120.3 %shard_map.37 = bf16[192,24,128]{2,1,0:T(8,128)(2,1)S(1)} custom-call(bf16[192,24,128]{2,1,0:T(8,128)(2,1)} %bitcast.5, bf16[32,24,128]{2,1,0:T(8,128)(2,1)S(1)} %bitcast.4, s32[1]{0:T(128)S(6)} %copy.5.rotor_step), custom_call_target="tpu_custom_call" | custom-call | tf_op jit(solution)/shard_map/pallas_call | solution.py:386
  121.9 1.0 copy.6
Async XLA Ops:
  0.7 0.9 copy-start

commit v3 on v2

--- a/solution.py
+++ b/solution.py
@@ -18,7 +18,7 @@
 RING = 64
 COLS = 16
 FAR = COLS // 2
-NEAR = 5
+NEAR = 4
 PARTS = 3
 GROUP = 8
 MESH = pl.DeviceIdType.MESH
@@ -422,7 +422,11 @@
         compiler_params=pltpu.CompilerParams(
             collective_id=0, has_side_effects=True, vmem_limit_bytes=52 * 1024 * 1024
         ),
-    )(state.reshape(ROWS, CELLS, LANES), diffusivity.reshape(PLANES, CELLS, LANES), rotor_step)
+    )(
+        pltpu.with_memory_space_constraint(state.reshape(ROWS, CELLS, LANES), pltpu.HBM),
+        pltpu.with_memory_space_constraint(diffusivity.reshape(PLANES, CELLS, LANES), pltpu.HBM),
+        rotor_step,
+    )
     return result.reshape(1, FIELDS, PLANES, CELLS, LANES)
 
 

time: 124 us -> 122 us (0.984)
  no operation moved by 1% of the time
where the time goes in v3:
time: 122 us
  Pallas kernels  120 us (98%)
    pallas_call x1, Pallas kernels, body(): pl.pallas_call(kernel, out_shape=jax.ShapeDtypeStruct((ROWS, CELLS, LANES...  120 us

profile of v3, /device:TPU:6, one launch (start us, length us, event | category | flops | bytes accessed | tf_op | source)
XLA Modules:
  0.0 121.7 jit_solution(5553033220246054066)
XLA Ops:
  0.7 120.0 %shard_map.37 = bf16[192,24,128]{2,1,0:T(8,128)(2,1)S(1)} custom-call(bf16[192,24,128]{2,1,0:T(8,128)(2,1)} %bitcast.4, bf16[32,24,128]{2,1,0:T(8,128)(2,1)} %bitcast.5, s32[1]{0:T(128)S(6)} %copy.5.rotor_step), custom_call_target="tpu_custom_call" | custom-call | tf_op jit(solution)/shard_map/pallas_call | solution.py:386
  120.7 1.0 copy.6

commit v4 on v3

--- a/solution.py
+++ b/solution.py
@@ -54,11 +54,10 @@
     state_hbm,
     diffusivity_hbm,
     rotor_step,
-    out,
+    base,
+    carried,
     cycles,
     rebuilt,
-    carried,
-    base,
     forward,
     back,
     spun,
@@ -340,17 +339,6 @@
         base[pl.ds(i * GROUP, GROUP)] = total
         return carry
 
-    def blend(part):
-        pltpu.make_async_copy(carried.at[part], carried.at[part], recv2.at[part]).wait()
-
-        def some(i, carry):
-            weight = side_weight(lax.rem(i, PLANES // GROUP) * GROUP + iota((GROUP, CELLS, LANES), 0))
-            rows = pl.ds(part * RING + i * GROUP, GROUP)
-            out[rows] = (base[rows] + weight * carried[part, pl.ds(i * GROUP, GROUP)].astype(F32)).astype(BF16)
-            return carry
-
-        lax.fori_loop(0, RING // GROUP, some, 0)
-
     transform(0)
 
     for copy in halos:
@@ -372,7 +360,7 @@
     for part in range(1, PARTS):
         transform(part)
     for part in range(PARTS):
-        blend(part)
+        pltpu.make_async_copy(carried.at[part], carried.at[part], recv2.at[part]).wait()
     for part in range(PARTS):
         pltpu.make_async_copy(cycles.at[part], cycles.at[part], send1.at[part]).wait()
         sent = rebuilt.at[part, pl.ds(0, RING - 1)]
@@ -383,16 +371,14 @@
     vmem = pl.BlockSpec(memory_space=pltpu.VMEM)
     hbm = pl.BlockSpec(memory_space=pltpu.HBM)
     block = (PARTS, RING, CELLS, LANES)
-    result = pl.pallas_call(
+    base, carried = pl.pallas_call(
         kernel,
-        out_shape=jax.ShapeDtypeStruct((ROWS, CELLS, LANES), BF16),
+        out_shape=(jax.ShapeDtypeStruct((ROWS, CELLS, LANES), F32), jax.ShapeDtypeStruct(block, BF16)),
         in_specs=[hbm, hbm, pl.BlockSpec(memory_space=pltpu.SMEM)],
-        out_specs=vmem,
+        out_specs=(vmem, vmem),
         scratch_shapes=[
             pltpu.VMEM(block, BF16),
             pltpu.VMEM(block, BF16),
-            pltpu.VMEM(block, BF16),
-            pltpu.VMEM((ROWS, CELLS, LANES), F32),
             pltpu.VMEM((2 * MODES, CYCLE), BF16),
             pltpu.VMEM((CYCLE, 2 * MODES), BF16),
             pltpu.VMEM((2 * MODES, LANES), BF16),
@@ -420,14 +406,18 @@
             pltpu.SemaphoreType.REGULAR((FAR + 1,)),
         ],
         compiler_params=pltpu.CompilerParams(
-            collective_id=0, has_side_effects=True, vmem_limit_bytes=52 * 1024 * 1024
+            collective_id=0, has_side_effects=True, vmem_limit_bytes=40 * 1024 * 1024
         ),
     )(
         pltpu.with_memory_space_constraint(state.reshape(ROWS, CELLS, LANES), pltpu.HBM),
         pltpu.with_memory_space_constraint(diffusivity.reshape(PLANES, CELLS, LANES), pltpu.HBM),
         rotor_step,
     )
-    return result.reshape(1, FIELDS, PLANES, CELLS, LANES)
+    middle = (iota((1, PLANES, 1, 1), 1).astype(F32) + 0.5) / PLANES
+    weight = jnp.where(lax.axis_index("ax") == 0, middle, 1.0 - middle)
+    shape = (FIELDS, PLANES, CELLS, LANES)
+    blended = base.reshape(shape) + weight * carried.reshape(shape).astype(F32)
+    return blended.astype(BF16)[None]
 
 
 def solution(mesh):

time: 122 us -> 122 us (level)
  other arithmetic: 0 us -> 1.4 us
    convert_element_type x0 -> x1, other arithmetic: none -> 1.39 us  [body(): return blended.astype(BF16)[None]]
where the time goes in v4:
time: 122 us
  Pallas kernels  120 us (98%)
  other arithmetic  1.4 us (1%)
    pallas_call x1, Pallas kernels, body(): pl.pallas_call(kernel, out_shape=(jax.ShapeDtypeStruct((ROWS, CELLS, LANE...  120 us

profile of v4, /device:TPU:6, one launch (start us, length us, event | category | flops | bytes accessed | tf_op | source)
XLA Modules:
  0.0 121.9 jit_solution(16766739337140786225)
XLA Ops:
  0.7 119.8 %shard_map.37 = (f32[192,24,128]{2,1,0:T(8,128)S(1)}, bf16[3,64,24,128]{3,2,1,0:T(8,128)(2,1)S(1)}) custom-call(bf16[192,24,128]{2,1,0:T(8,128)(2,1)} %bitcast.7, bf16[32,24,128]{2,1,0:T(8,128)(2,1)} %bitcast.8, s32[1]{0:T(128)S(6)} %copy.4.rotor_step), custom_call_target="tpu_custom_call" | custom-call | tf_op jit(solution)/shard_map/pallas_call | solution.py:374
  120.5 1.4 %fusion.1 = bf16[1,6,32,24,128]{4,3,2,1,0:T(8,128)(2,1)} fusion(f32[1,6,32,24,128]{4,3,2,1,0:T(8,128)S(1)} %bitcast.5, bf16[1,6,32,24,128]{4,3,2,1,0:T(8,128)(2,1)S(1)} %bitcast.6, f32[32]{0:T(128)S(1)} %broadcast_select_fusion), kind=kLoop, calls=%fused_computation.2 | loop fusion | flops 2359296 | bytes 4718720 | tf_op jit(solution)/shard_map/convert_element_type | solution.py:420
  (1 shorter events, 0.0 us)
